TPU v7x, 32 devices: a whole 2x2x4 slice. The times are simulated.
32 devices in a mesh: grp: 4 (over x, core), wide: 8 (over z, y).
Axes of the slice: x: 2, y: 2, z: 4, core: 2. Of those that a mesh axis runs over, the one named last changes fastest.
Arguments:
- anchor_states: bfloat16 [4096, 1024], P(('wide', 'grp')), may hold values from -6 to 6
- key_weight: bfloat16 [1024, 1024], P(None, 'grp'), may hold values from -0.1875 to 0.1875
- value_weight: bfloat16 [1024, 1024], P(None, 'grp'), may hold values from -0.1875 to 0.1875
- panel_query: bfloat16 [8192, 1024], P(('wide', 'grp')), may hold values from -160 to 160
- cell_list: int32 [64, 4], P('wide'), may hold values from 0 to 3, as said below
- cell_count: int32 [64], P('wide'), may hold values from 1 to 4, as said below
- norm_gain: float32 [1024], replicated, may hold values from 0.1 to 1.9
- up_weight: bfloat16 [1024, 512], replicated, may hold values from -0.1875 to 0.1875
- flux_weight: bfloat16 [4, 512], replicated, may hold values from -0.25 to 0.25
Outputs:
- flux: float32 [4, 8192], P(None, ('wide', 'grp'))
Inputs may be any that keep to these rules, and one draw needn't show every extreme that they name: `cell_list`: the entries of a row are distinct cell blocks of that panel block's region; entries past cell_count are not used. `cell_count`: every region has a panel block whose list uses all 4 slots.
All inputs are finite; a program needn't handle non-finite values.
Results may differ from a plain program's by a relative error of at most 0.007.
Values may be sent and summed in bfloat16 or wider, within the bound.
A program may use at most 64 MiB of HBM per device.

v0:
```python
import functools
import math

import jax
import jax.numpy as jnp
from jax import lax
from jax.experimental import pallas as pl
from jax.experimental.pallas import tpu as pltpu
from jax.sharding import PartitionSpec as P

BLK = 128
LMAX = 4
HD = 64
LANES = 128
ONES = 16
STEP = 256
MESH = pl.DeviceIdType.MESH


def kernel(
    n_wide,
    n_grp,
    anchor_hbm,
    key_hbm,
    value_hbm,
    query_hbm,
    list_ref,
    count_ref,
    gain_ref,
    up_hbm,
    flux_w_ref,
    flux_ref,
    anchors,
    weights,
    keys,
    values,
    region_query,
    outgoing,
    attended,
    query,
    up,
    back,
    local_sem,
    anchor_send,
    anchor_recv,
    forward_send,
    query_send,
    query_recv,
    out_send,
    out_recv,
    back_send,
    back_recv,
):
    w = lax.axis_index("wide")
    g = lax.axis_index("grp")
    slabs = n_wide // n_grp
    slab = region_query.shape[1]
    cols = region_query.shape[2]
    pairs = cols // LANES
    chips = n_grp // 2
    core = g % 2
    chip = g // 2
    sibling = chip * 2 + 1 - core
    home = w // slabs
    here = home == g

    loads = [
        pltpu.make_async_copy(anchor_hbm, anchors.at[g], local_sem.at[0]),
        pltpu.make_async_copy(key_hbm, weights.at[:, pl.ds(0, cols)], local_sem.at[1]),
        pltpu.make_async_copy(value_hbm, weights.at[:, pl.ds(cols, cols)], local_sem.at[2]),
        pltpu.make_async_copy(query_hbm, query, local_sem.at[3]),
        pltpu.make_async_copy(up_hbm, up, local_sem.at[4]),
    ]
    for load in loads:
        load.start()

    barrier = pltpu.get_barrier_semaphore()

    def greet(wide, grp):
        pl.semaphore_signal(barrier, inc=1, device_id=(grp, wide), device_id_type=MESH)

    @pl.loop(1, n_grp)
    def _(i):
        greet(w, (g + i) % n_grp)

    @pl.loop(0, n_wide)
    def _(i):
        region = g * slabs + i // n_grp
        head = i % n_grp

        @pl.when(jnp.logical_or(region != w, head != g))
        def _():
            greet(region, head)

        @pl.when(jnp.logical_or(i != w, home != g))
        def _():
            greet(i, home)

    @pl.loop(1, n_wide)
    def _(i):
        greet((w + i) % n_wide, g)

    pl.semaphore_wait(barrier, n_grp - 2 + 3 * n_wide - 2 * here.astype(jnp.int32))

    def anchor_copy(grp, index):
        return pltpu.make_async_remote_copy(
            src_ref=anchor_hbm,
            dst_ref=anchors.at[g],
            send_sem=anchor_send.at[index],
            recv_sem=anchor_recv.at[g],
            device_id=(grp, w),
            device_id_type=MESH,
        )

    for j in range(1, chips):
        anchor_copy(((chip + j) % chips) * 2 + core, j).start()
    anchor_copy(sibling, 0).start()

    def query_source(i):
        s = i // n_grp
        head = i % n_grp
        return query_hbm.at[
            pl.ds(pl.multiple_of(s * slab, 16), slab), pl.ds(pl.multiple_of(head * cols, LANES), cols)
        ]

    def query_copy(i):
        return pltpu.make_async_remote_copy(
            src_ref=query_source(i),
            dst_ref=region_query.at[w],
            send_sem=query_send.at[i],
            recv_sem=query_recv.at[w],
            device_id=(i % n_grp, g * slabs + i // n_grp),
            device_id_type=MESH,
        )

    def is_self(i):
        return jnp.logical_and(g * slabs + i // n_grp == w, i % n_grp == g)

    def send_queries(near):
        @pl.loop(0, n_wide)
        def _(i):
            chosen = ((i % n_grp) // 2 == chip) if near else ((i % n_grp) // 2 != chip)

            if near:

                @pl.when(is_self(i))
                def _():
                    pltpu.make_async_copy(
                        query_source(i), region_query.at[w], query_recv.at[w]
                    ).start()

            @pl.when(jnp.logical_and(chosen, jnp.logical_not(is_self(i))))
            def _():
                query_copy(i).start()

    send_queries(True)

    low = lax.broadcasted_iota(jnp.int32, (BLK, LANES), 1) < HD

    def project(cell):
        both = jnp.dot(anchors[cell], weights[...], preferred_element_type=jnp.float32)
        rows = pl.ds(pl.multiple_of(cell * BLK, BLK), BLK)
        for j in range(pairs):
            k = both[:, j * LANES : (j + 1) * LANES]
            keys[j, 0, rows, :] = jnp.where(low, k, 0.0).astype(jnp.bfloat16)
            keys[j, 1, rows, :] = jnp.where(low, 0.0, k).astype(jnp.bfloat16)
        turned = both[:, cols:].T.astype(jnp.bfloat16)
        for h in range(2 * pairs):
            values[h, :HD, rows] = turned[h * HD : (h + 1) * HD]

    def wait_anchor(cell):
        pltpu.make_async_copy(anchors.at[cell], anchors.at[cell], anchor_recv.at[cell]).wait()

    def forward_copy(cell, j):
        return pltpu.make_async_remote_copy(
            src_ref=anchors.at[cell],
            dst_ref=anchors.at[cell],
            send_sem=forward_send.at[j],
            recv_sem=anchor_recv.at[cell],
            device_id=(sibling, w),
            device_id_type=MESH,
        )

    def across(j):
        return (chip + chips - j) % chips

    values[:, HD:, :] = jnp.ones((2 * pairs, ONES, values.shape[2]), jnp.bfloat16)
    for load in loads[:3]:
        load.wait()
    project(g)
    wait_anchor(sibling)
    project(sibling)
    for j in range(1, chips):
        cell = across(j) * 2 + core
        wait_anchor(cell)
        forward_copy(cell, j).start()
    send_queries(False)
    for j in range(1, chips):
        project(across(j) * 2 + core)
    for j in range(1, chips):
        cell = across(j) * 2 + 1 - core
        wait_anchor(cell)
        project(cell)

    scale = math.log2(math.e) / math.sqrt(HD)
    group = STEP // slab
    blocks = STEP // BLK
    nt = (((1,), (1,)), ((), ()))

    def out_copy(p):
        return pltpu.make_async_remote_copy(
            src_ref=outgoing.at[p],
            dst_ref=attended.at[g, w % slabs],
            send_sem=out_send.at[p],
            recv_sem=out_recv.at[g, w % slabs],
            device_id=(home, p),
            device_id_type=MESH,
        )

    half = n_wide // 2

    def far(p):
        return p // half != w // half

    def hops(p):
        return jnp.logical_and(far(p), home // 2 != chip)

    def hop_copy(p):
        return pltpu.make_async_remote_copy(
            src_ref=outgoing.at[p],
            dst_ref=back.at[w],
            send_sem=out_send.at[p],
            recv_sem=back_recv.at[w],
            device_id=(g, p),
            device_id_type=MESH,
        )

    def back_copy(r):
        return pltpu.make_async_remote_copy(
            src_ref=back.at[r],
            dst_ref=attended.at[g, r % slabs],
            send_sem=back_send.at[r],
            recv_sem=out_recv.at[g, r % slabs],
            device_id=(r // slabs, w),
            device_id_type=MESH,
        )

    def passed_on(r):
        return jnp.logical_and(far(r), (r // slabs) // 2 != chip)

    def flipped(index, k, count):
        bit = 1
        while bit < count:
            index = index + ((k // bit) % 2) * bit * (1 - 2 * ((index // bit) % 2))
            bit *= 2
        return index

    def listed(block):
        used = count_ref[block]
        bias = []
        for c in range(n_grp):
            live = jnp.logical_and(list_ref[0, block] == c, used > 0)
            for slot in range(1, LMAX):
                live = jnp.logical_or(live, jnp.logical_and(list_ref[slot, block] == c, used > slot))
            bias.append(jnp.full((1, BLK), jnp.where(live, 0.0, -jnp.inf), jnp.float32))
        return bias

    def attend(a):
        base = a * group
        biases = [listed(a * blocks + i) for i in range(blocks)]
        bias = [jnp.concatenate([one[c] for one in biases], axis=1) for c in range(n_grp)]
        for m in range(group):
            p = base + m
            pltpu.make_async_copy(region_query.at[p], region_query.at[p], query_recv.at[p]).wait()
        queries = region_query[pl.ds(base, group)].reshape(STEP, cols)
        heads = []
        for j in range(pairs):
            q = queries[:, j * LANES : (j + 1) * LANES]
            for i in range(2):
                scores = lax.dot_general(keys[j, i], q, nt, preferred_element_type=jnp.float32)
                cells = [scores[c * BLK : (c + 1) * BLK] for c in range(n_grp)]
                top = None
                for c in range(n_grp):
                    one = jnp.max(cells[c], axis=0, keepdims=True) * scale + bias[c]
                    top = one if top is None else jnp.maximum(top, one)
                expo = jnp.concatenate(
                    [
                        jnp.exp2(cells[c] * scale + (bias[c] - top)).astype(jnp.bfloat16)
                        for c in range(n_grp)
                    ],
                    axis=0,
                )
                summed = jnp.dot(values[2 * j + i], expo, preferred_element_type=jnp.float32)
                heads.append(summed[:HD] * (1.0 / summed[HD : HD + 1]))
        joined = jnp.concatenate(heads, axis=0).T.astype(jnp.bfloat16)
        outgoing[pl.ds(base, group)] = joined.reshape(group, slab, cols)
        for m in range(group):
            p = base + m
            mine = jnp.logical_and(p == w, here)

            @pl.when(mine)
            def _():
                pltpu.make_async_copy(
                    outgoing.at[p], attended.at[g, w % slabs], out_recv.at[g, w % slabs]
                ).start()

            @pl.when(hops(p))
            def _():
                hop_copy(p).start()

            @pl.when(jnp.logical_not(jnp.logical_or(mine, hops(p))))
            def _():
                out_copy(p).start()

    groups = n_wide // group

    @pl.loop(0, groups)
    def _(t):
        attend(flipped(w // group, t, groups))

    @pl.loop(half, n_wide)
    def _(k):
        r = flipped(w, k, n_wide)

        @pl.when(passed_on(r))
        def _():
            pltpu.make_async_copy(back.at[r], back.at[r], back_recv.at[r]).wait()
            back_copy(r).start()

    for load in loads[3:]:
        load.wait()
    for h in range(n_grp):
        for s in range(slabs):
            pltpu.make_async_copy(
                attended.at[h, s], attended.at[h, s], out_recv.at[h, s]
            ).wait()
    rows = query.shape[0]
    dim = query.shape[1]
    stream = []
    square = jnp.zeros((rows, 1), jnp.float32)
    for h in range(n_grp):
        part = query[:, h * cols : (h + 1) * cols].astype(jnp.float32) + attended[h].reshape(
            rows, cols
        ).astype(jnp.float32)
        square = square + jnp.sum(part * part, axis=-1, keepdims=True)
        stream.append(part)
    factor = lax.rsqrt(square / dim + 1e-06)
    normed = jnp.concatenate(
        [
            (stream[h] * factor * gain_ref[:, h * cols : (h + 1) * cols]).astype(jnp.bfloat16)
            for h in range(n_grp)
        ],
        axis=1,
    )
    hidden = jax.nn.gelu(
        jnp.dot(normed, up[...], preferred_element_type=jnp.float32), approximate=True
    ).astype(jnp.bfloat16)
    flux_ref[...] = lax.dot_general(flux_w_ref[...], hidden, nt, preferred_element_type=jnp.float32)

    for j in range(1, chips):
        anchor_copy(((chip + j) % chips) * 2 + core, j).wait_send()
        forward_copy(across(j) * 2 + core, j).wait_send()
    anchor_copy(sibling, 0).wait_send()

    @pl.loop(0, n_wide)
    def _(i):
        @pl.when(jnp.logical_not(is_self(i)))
        def _():
            query_copy(i).wait_send()

        @pl.when(jnp.logical_not(jnp.logical_and(i == w, here)))
        def _():
            out_copy(i).wait_send()

        @pl.when(passed_on(i))
        def _():
            back_copy(i).wait_send()


def body(n_wide, n_grp, anchor, key_w, value_w, query, cell_list, cell_count, gain, up, flux_w):
    rows, dim = query.shape
    cols = key_w.shape[1]
    slabs = n_wide // n_grp
    slab = rows // slabs
    cells = n_grp
    pairs = cols // LANES
    any_space = pl.BlockSpec(memory_space=pl.ANY)
    vmem = pl.BlockSpec(memory_space=pltpu.VMEM)
    smem = pl.BlockSpec(memory_space=pltpu.SMEM)
    bf16 = jnp.bfloat16
    dma = pltpu.SemaphoreType.DMA
    return pl.pallas_call(
        functools.partial(kernel, n_wide, n_grp),
        out_shape=jax.ShapeDtypeStruct((flux_w.shape[0], rows), jnp.float32),
        in_specs=[any_space] * 4 + [smem] * 2 + [vmem, any_space, vmem],
        out_specs=vmem,
        scratch_shapes=[
            pltpu.VMEM((cells, BLK, dim), bf16),
            pltpu.VMEM((dim, 2 * cols), bf16),
            pltpu.VMEM((pairs, 2, cells * BLK, LANES), bf16),
            pltpu.VMEM((2 * pairs, HD + ONES, cells * BLK), bf16),
            pltpu.VMEM((n_wide, slab, cols), bf16),
            pltpu.VMEM((n_wide, slab, cols), bf16),
            pltpu.VMEM((n_grp, slabs, slab, cols), bf16),
            pltpu.VMEM((rows, dim), bf16),
            pltpu.VMEM(up.shape, bf16),
            pltpu.VMEM((n_wide, slab, cols), bf16),
            dma((5,)),
            dma((max(n_grp // 2, 1),)),
            dma((n_grp,)),
            dma((max(n_grp // 2, 1),)),
            dma((n_wide,)),
            dma((n_wide,)),
            dma((n_wide,)),
            dma((n_grp, slabs)),
            dma((n_wide,)),
            dma((n_wide,)),
        ],
        compiler_params=pltpu.CompilerParams(
            collective_id=0, has_side_effects=True, vmem_limit_bytes=56 * 1024 * 1024
        ),
        cost_estimate=pl.CostEstimate(flops=3 * 10**9, bytes_accessed=6 * 10**6, transcendentals=0),
    )(anchor, key_w, value_w, query, cell_list.T, cell_count, gain[None, :], up, flux_w)


def solution(mesh):
    in_specs = (
        P(("wide", "grp"), None),
        P(None, "grp"),
        P(None, "grp"),
        P(("wide", "grp"), None),
        P("wide", None),
        P("wide"),
        P(),
        P(),
        P(),
    )
    out_specs = P(None, ("wide", "grp"))
    step = functools.partial(body, mesh.shape["wide"], mesh.shape["grp"])
    return jax.shard_map(step, mesh=mesh, in_specs=in_specs, out_specs=out_specs, check_vma=False)
```

profile of v0, /device:TPU:7, one launch (start us, length us, event | category | flops | bytes accessed | tf_op | source)
XLA Modules:
  0.0 51.1 jit_solution(10840522331748513850)
XLA Ops:
  0.0 49.8 %shard_map.91 = f32[4,256]{1,0:T(4,128)} custom-call(bf16[128,1024]{1,0:T(8,128)(2,1)} %anchor_hbm.1, bf16[1024,256]{1,0:T(8,128)(2,1)} %key_hbm.1, bf16[1024,256]{1,0:T(8,128)(2,1)} %value_hbm.1, bf16[256,1024]{1,0:T(8,128)(2,1)} %query_hbm.1, s32[4,8]{1,0:T(4,128)} %bitcast.3, s32[8]{0:T(128)} %count_ref.1, f32[1,1024]{1,0:T(1,128)} %bitcast.2, ...), custom_call_target="tpu_custom_call" | custom-call | flops 3000000000 | bytes 6000000 | tf_op jit(solution)/shard_map/pallas_call | solution.py:392
  49.8 1.3 %copy.11 = f32[4,256]{1,0:T(4,128)} copy(f32[4,256]{1,0:T(4,128)} %shard_map.91) | data formatting | bytes 8192
where the time goes:
time: 51.3 us; the launch traced here: 51.1 us
  Pallas kernels  49.8 us (97%)
  local copies, waits for them, and re-layouts  1.28 us (2%)
    pallas_call x1, Pallas kernels, body(): pl.pallas_call(functools.partial(kernel, n_wide, n_grp), out_shape=jax.Sh...  49.8 us
    unnamed x1, local copies, waits for them, and re-layouts  1.28 us

commit v1 on v0

--- a/solution.py
+++ b/solution.py
@@ -136,24 +136,15 @@
     def is_self(i):
         return jnp.logical_and(g * slabs + i // n_grp == w, i % n_grp == g)
 
-    def send_queries(near):
-        @pl.loop(0, n_wide)
-        def _(i):
-            chosen = ((i % n_grp) // 2 == chip) if near else ((i % n_grp) // 2 != chip)
-
-            if near:
-
-                @pl.when(is_self(i))
-                def _():
-                    pltpu.make_async_copy(
-                        query_source(i), region_query.at[w], query_recv.at[w]
-                    ).start()
-
-            @pl.when(jnp.logical_and(chosen, jnp.logical_not(is_self(i))))
-            def _():
-                query_copy(i).start()
-
-    send_queries(True)
+    @pl.loop(0, n_wide)
+    def _(i):
+        @pl.when(is_self(i))
+        def _():
+            pltpu.make_async_copy(query_source(i), region_query.at[w], query_recv.at[w]).start()
+
+        @pl.when(jnp.logical_not(is_self(i)))
+        def _():
+            query_copy(i).start()
 
     low = lax.broadcasted_iota(jnp.int32, (BLK, LANES), 1) < HD
 
@@ -194,7 +185,6 @@
         cell = across(j) * 2 + core
         wait_anchor(cell)
         forward_copy(cell, j).start()
-    send_queries(False)
     for j in range(1, chips):
         project(across(j) * 2 + core)
     for j in range(1, chips):

time: 51.3 us -> 49.2 us (0.959)
  Pallas kernels: 49.8 us -> 47.7 us
    pallas_call x1, Pallas kernels: 49.8 us -> 47.7 us  [body(): pl.pallas_call(functools.partial(kernel, n_wide, n_grp), out_shape=jax.Sh...]
where the time goes in v1:
time: 49.2 us; the launch traced here: 49 us
  Pallas kernels  47.7 us (97%)
  local copies, waits for them, and re-layouts  1.28 us (3%)
    pallas_call x1, Pallas kernels, body(): pl.pallas_call(functools.partial(kernel, n_wide, n_grp), out_shape=jax.Sh...  47.7 us
    unnamed x1, local copies, waits for them, and re-layouts  1.28 us

profile of v1, /device:TPU:7, one launch (start us, length us, event | category | flops | bytes accessed | tf_op | source)
XLA Modules:
  0.0 49.0 jit_solution(5447956600910617397)
XLA Ops:
  0.0 47.7 %shard_map.91 = f32[4,256]{1,0:T(4,128)} custom-call(bf16[128,1024]{1,0:T(8,128)(2,1)} %anchor_hbm.1, bf16[1024,256]{1,0:T(8,128)(2,1)} %key_hbm.1, bf16[1024,256]{1,0:T(8,128)(2,1)} %value_hbm.1, bf16[256,1024]{1,0:T(8,128)(2,1)} %query_hbm.1, s32[4,8]{1,0:T(4,128)} %bitcast.3, s32[8]{0:T(128)} %count_ref.1, f32[1,1024]{1,0:T(1,128)} %bitcast.2, ...), custom_call_target="tpu_custom_call" | custom-call | flops 3000000000 | bytes 6000000 | tf_op jit(solution)/shard_map/pallas_call | solution.py:382
  47.7 1.3 %copy.11 = f32[4,256]{1,0:T(4,128)} copy(f32[4,256]{1,0:T(4,128)} %shard_map.91) | data formatting | bytes 8192
